TPU v7x, 32 devices: a whole 2x2x4 slice. The times are simulated.
32 devices in a mesh: dp: 16 (over z, y, x), tensor: 2 (over core).
Axes of the slice: x: 2, y: 2, z: 4, core: 2. Of those that a mesh axis runs over, the one named last changes fastest.
Arguments:
- stream: bfloat16 [10240, 1024], P(('dp', 'tensor')), may hold values from -24 to 24
- counts: int32 [32], P('dp'), may hold values from 16 to 256
- cotangent: bfloat16 [10240, 1024], P(('dp', 'tensor')), may hold values from -6 to 6
- w_qkv: bfloat16 [3, 1024, 1024], P(None, 'dp', 'tensor'), may hold values from -0.1875 to 0.1875
- b_qv: float32 [2, 1024], replicated, may hold values from -1.5 to 1.5
- w_out: bfloat16 [1024, 1024], P('tensor', 'dp'), may hold values from -0.75 to 0.75
- b_out: float32 [1024], replicated, may hold values from -1.8 to 1.8
- w_fc1: bfloat16 [1024, 4096], P('dp', 'tensor'), may hold values from -0.35 to 0.35
- b_fc1: float32 [4096], replicated, may hold values from -3 to 3
- w_fc2: bfloat16 [4096, 1024], P('tensor', 'dp'), may hold values from -0.09375 to 0.09375
- b_fc2: float32 [1024], replicated, may hold values from -1.8 to 1.8
- gain_one: float32 [1024], replicated, may hold values from 0.25 to 1.75
- shift_one: float32 [1024], replicated, may hold values from -1.8 to 1.8
- gain_two: float32 [1024], replicated, may hold values from 0.25 to 1.75
- shift_two: float32 [1024], replicated, may hold values from -1.8 to 1.8
Outputs:
- activations: bfloat16 [10240, 1024], P(('dp', 'tensor'))
- grad_input: float32 [10240, 1024], P(('dp', 'tensor'))
- grad_w_qkv: float32 [3, 1024, 1024], P(None, 'dp', 'tensor')
- grad_b_qv: float32 [2, 1024], P(None, ('dp', 'tensor'))
- grad_w_out: float32 [1024, 1024], P('tensor', 'dp')
- grad_b_out: float32 [1024], P(('dp', 'tensor'))
- grad_w_fc1: float32 [1024, 4096], P('dp', 'tensor')
- grad_b_fc1: float32 [4096], P(('dp', 'tensor'))
- grad_w_fc2: float32 [4096, 1024], P('tensor', 'dp')
- grad_b_fc2: float32 [1024], P(('dp', 'tensor'))
- grad_gain_one: float32 [1024], P(('dp', 'tensor'))
- grad_shift_one: float32 [1024], P(('dp', 'tensor'))
- grad_gain_two: float32 [1024], P(('dp', 'tensor'))
- grad_shift_two: float32 [1024], P(('dp', 'tensor'))
- rms_stats: float32 [5], replicated
All inputs are finite; a program needn't handle non-finite values.
Results may differ from a plain program's by a relative error of at most 0.02.
Values may be sent and summed in bfloat16 or wider, within the bound.
A program may use at most 128 MiB of HBM per device.

v0:
```python
import jax
import jax.numpy as jnp
from jax import lax
from jax.experimental import pallas as pl
from jax.experimental.pallas import tpu as pltpu
from jax.sharding import PartitionSpec as P

HD = 64
BUFFER = 64
SLOTS = 320


eps_norm = 1e-06


MESH = pl.DeviceIdType.MESH


class Place:
    def __init__(self):
        dp = lax.axis_index("dp")
        self.t = lax.axis_index("tensor")
        self.z, self.y, self.x = dp // 4, (dp // 2) % 2, dp % 2
        self.side = self.z // 2
        self.w = self.z + self.side * (3 - 2 * self.z)
        self.step = 1 - 2 * self.side
        self.dp = dp

    def order(self, k):
        o = (self.w, 1 - self.w, 2, 3)[k]
        return 3 * self.side + self.step * o

    def chip(self, z, y, x):
        return z * 4 + y * 2 + x

    def inward(self):
        return (self.chip(self.z + self.step, self.y, self.x), self.t)

    def outward(self):
        return (self.chip(self.z - self.step, self.y, self.x), self.t)

    def across_x(self):
        return (self.chip(self.z, self.y, 1 - self.x), self.t)

    def across_y(self):
        return (self.chip(self.z, 1 - self.y, self.x), self.t)

    def near(self):
        return (self.chip(self.z + 1 - 2 * (self.z % 2), self.y, self.x), self.t)

    def far(self):
        return (self.chip((self.z + 2) % 4, self.y, self.x), self.t)

    def twin(self):
        return (self.dp, 1 - self.t)


def greet(at):
    barrier = pltpu.get_barrier_semaphore()
    for other in (at.across_x(), at.across_y(), at.inward(), at.twin(), at.far()):
        pl.semaphore_signal(barrier, inc=1, device_id=other, device_id_type=MESH)

    @pl.when(at.w == 1)
    def _():
        pl.semaphore_signal(barrier, inc=1, device_id=at.outward(), device_id_type=MESH)


def enter(at):
    pl.semaphore_wait(pltpu.get_barrier_semaphore(), 5 + at.w)


def settle(ref, sem, at, sent):
    copy = pltpu.make_async_remote_copy(
        src_ref=ref, dst_ref=ref, send_sem=sem, recv_sem=sem, device_id=at.twin(), device_id_type=MESH
    )
    if sent:
        copy.wait_send()
    else:
        copy.wait_recv()


class Gather:
    def __init__(self, at, full, shard, pieces, send, recv):
        self.at, self.full, self.shard, self.pieces, self.send, self.recv = at, full, shard, pieces, send, recv

    def rows(self, p, z, y, x, part=None):
        c0, c1 = self.pieces[p]
        start, size = self.at.chip(z, y, x) * self.shard, self.shard
        if part is not None:
            size = self.shard // 2
            start = start + part * size
        return self.full.at[pl.ds(pl.multiple_of(start, size), size), pl.ds(c0, c1 - c0)]

    def copy(self, p, ref, s, r, other):
        return pltpu.make_async_remote_copy(
            src_ref=ref,
            dst_ref=ref,
            send_sem=self.send.at[s],
            recv_sem=self.recv.at[p, r],
            device_id=other,
            device_id_type=MESH,
        )

    def z_in(self, p, z):
        return self.copy(p, self.rows(p, z, self.at.y, self.at.x), 1, z, self.at.inward())

    def z_out(self, p, z):
        return self.copy(p, self.rows(p, z, self.at.y, self.at.x), 1, z, self.at.outward())

    def x_full(self, p, z):
        return self.copy(p, self.rows(p, z, self.at.y, self.at.x), 0, 4 + z, self.at.across_x())

    def y_full(self, p, z):
        return self.copy(p, self.rows(p, z, self.at.y, self.at.x), 0, 8 + z, self.at.across_y())

    def x_half(self, p, z):
        return self.copy(p, self.rows(p, z, 1 - self.at.y, self.at.x, 1), 0, 12, self.at.across_x())

    def y_half(self, p, z):
        return self.copy(p, self.rows(p, z, self.at.y, 1 - self.at.x, 0), 0, 12, self.at.across_y())

    def arrived(self, p, kind, z):
        at = self.at
        ref = (
            lambda: self.rows(p, z, at.y, at.x),
            lambda: self.rows(p, z, at.y, 1 - at.x),
            lambda: self.rows(p, z, 1 - at.y, at.x),
        )[kind]()
        settle(ref, self.recv.at[p, 4 * kind + z], at, False)

    def line(self, p, k, w):
        at = self.at

        @pl.when(at.w == w)
        def _():
            z = at.order(k)
            if k > 0:
                self.arrived(p, 0, z)
            if k == 0 or (k == 1 and w == 1):
                self.z_in(p, z).start()
            if w == 1 and k != 1:
                self.z_out(p, z).start()
            self.x_full(p, z).start()
            self.y_full(p, z).start()

    def plane(self, p, k):
        z = self.at.order(k)
        self.arrived(p, 1, z)
        self.y_half(p, z).start()
        self.arrived(p, 2, z)
        self.x_half(p, z).start()

    def finish(self, p):
        c0, c1 = self.pieces[p]
        settle(self.full.at[0 : 4 * self.shard, c0:c1], self.recv.at[p, 12], self.at, False)

    def drain(self):
        n = sum(c1 - c0 for c0, c1 in self.pieces)
        settle(self.full.at[0 : 12 * self.shard, 0:n], self.send.at[0], self.at, True)
        for w, blocks in ((0, 1), (1, 5)):

            @pl.when(self.at.w == w)
            def _(blocks=blocks):
                settle(self.full.at[0 : blocks * self.shard, 0:n], self.send.at[1], self.at, True)


class Scatter:
    def __init__(self, at, full, shard, pieces, xh, yh, xf, yf, zl, send, recv):
        self.at, self.full, self.shard, self.pieces = at, full, shard, pieces
        self.xh, self.yh, self.xf, self.yf, self.zl = xh, yh, xf, yf, zl
        self.send, self.recv = send, recv

    def cols(self, p):
        c0, c1 = self.pieces[p]
        return pl.ds(c0, c1 - c0)

    def rows(self, p, z, y, x, part=None):
        start, size = self.at.chip(z, y, x) * self.shard, self.shard
        if part is not None:
            size = self.shard // 2
            start = start + part * size
        ref, c0, c1 = self.full(p)
        return ref.at[pl.ds(pl.multiple_of(start, size), size), pl.ds(c0, c1 - c0)]

    def copy(self, p, src, dst, r, other):
        return pltpu.make_async_remote_copy(
            src_ref=src,
            dst_ref=dst,
            send_sem=self.send.at[0],
            recv_sem=self.recv.at[p, r],
            device_id=other,
            device_id_type=MESH,
        )

    def x_half(self, p, z):
        at = self.at
        return self.copy(
            p, self.rows(p, z, 1 - at.y, 1 - at.x, 0), self.xh.at[z, :, self.cols(p)], z, at.across_x()
        )

    def y_half(self, p, z):
        at = self.at
        return self.copy(
            p, self.rows(p, z, 1 - at.y, 1 - at.x, 1), self.yh.at[z, :, self.cols(p)], z, at.across_y()
        )

    def x_full(self, p, z):
        at = self.at
        return self.copy(
            p, self.rows(p, z, at.y, 1 - at.x), self.xf.at[z, :, self.cols(p)], 4 + z, at.across_x()
        )

    def y_full(self, p, z):
        at = self.at
        return self.copy(
            p, self.rows(p, z, 1 - at.y, at.x), self.yf.at[z, :, self.cols(p)], 4 + z, at.across_y()
        )

    def z_in(self, p, z, slot):
        at = self.at
        return self.copy(
            p, self.rows(p, z, at.y, at.x), self.zl.at[slot, :, self.cols(p)], 8 + slot, at.inward()
        )

    def z_out(self, p, z, slot):
        at = self.at
        return self.copy(
            p, self.rows(p, z, at.y, at.x), self.zl.at[slot, :, self.cols(p)], 8 + slot, at.outward()
        )

    def begin(self, p, k):
        z = self.at.order(k)
        self.x_half(p, z).start()
        self.y_half(p, z).start()

    def plane(self, p, k):
        at = self.at
        z = at.order(k)
        settle(self.xf.at[z, :, self.cols(p)], self.recv.at[p, z], at, False)
        ref = self.rows(p, z, 1 - at.y, at.x, 0)
        ref[...] = ref[...] + self.xh[z, :, self.cols(p)]
        self.y_full(p, z).start()
        ref = self.rows(p, z, at.y, 1 - at.x, 1)
        ref[...] = ref[...] + self.yh[z, :, self.cols(p)]
        self.x_full(p, z).start()

    def wait_line(self, p, z, slot):
        self.z_in(p, z, slot).wait_recv()

    def line(self, p, k, w, out):
        at = self.at

        @pl.when(at.w == w)
        def _():
            z = at.order(k)
            full, c0, c1 = self.full(p)
            settle(full.at[0 : 2 * self.shard, c0:c1], self.recv.at[p, 4 + z], at, False)
            ref = self.rows(p, z, at.y, at.x)
            parts = [self.xf.at[z, :, self.cols(p)], self.yf.at[z, :, self.cols(p)]]
            if w == 1:
                self.wait_line(p, z, z)
                parts.append(self.zl.at[z, :, self.cols(p)])
            if k == 0:
                self.wait_line(p, z, 4)
                parts.append(self.zl.at[4, :, self.cols(p)])
            total = ref[...].astype(jnp.float32)
            for part in parts:
                total = total + part[...].astype(jnp.float32)
            if k == 0:
                out(total)
            else:
                ref[...] = total.astype(jnp.bfloat16)
                if w == 0 or k == 3:
                    self.z_in(p, z, z).start()
                elif k == 2:
                    self.z_in(p, z, 4).start()
                else:
                    self.z_out(p, z, 4).start()

    def drain(self, ref):
        settle(ref, self.send.at[0], self.at, True)


class PairGather:
    def __init__(self, at, full, shard, columns, sources, send, recv):
        self.at, self.full, self.shard, self.columns, self.sources = at, full, shard, columns, sources
        self.send, self.recv = send, recv

    def far_x(self, h):
        return self.at.x if h == 0 else 1 - self.at.x

    def rows(self, m, z, y, x):
        c0, n = self.columns[m]
        start = self.at.chip(z, y, x) * self.shard
        return self.full.at[pl.ds(pl.multiple_of(start, self.shard), self.shard), pl.ds(c0, n)]

    def copy(self, m, src, dst, s, r, other):
        return pltpu.make_async_remote_copy(
            src_ref=src,
            dst_ref=dst,
            send_sem=self.send.at[s],
            recv_sem=self.recv.at[m, r],
            device_id=other,
            device_id_type=MESH,
        )

    def x_copy(self, m):
        at = self.at
        c0, n = self.columns[m]
        src = self.sources[m].at[:, pl.ds(pl.multiple_of((1 - at.x) * n, n), n)]
        return self.copy(m, src, self.rows(m, at.z, at.y, at.x), 0, 8, at.across_x())

    def z_in(self, m, h, z):
        ref = self.rows(m, z, self.at.y, self.far_x(h))
        return self.copy(m, ref, ref, 1, 4 * h + z, self.at.inward())

    def z_out(self, m, h, z):
        ref = self.rows(m, z, self.at.y, self.far_x(h))
        return self.copy(m, ref, ref, 1, 4 * h + z, self.at.outward())

    def y_copy(self, m, h, z):
        ref = self.rows(m, z, self.at.y, self.far_x(h))
        return self.copy(m, ref, ref, 0, 9, self.at.across_y())

    def line(self, m, h, k, w):
        at = self.at

        @pl.when(at.w == w)
        def _():
            z = at.order(k)
            ref = self.rows(m, z, at.y, self.far_x(h))
            if k > 0:
                settle(ref, self.recv.at[m, 4 * h + z], at, False)
            elif h == 1:
                settle(ref, self.recv.at[m, 8], at, False)
            if k == 0 or (k == 1 and w == 1):
                self.z_in(m, h, z).start()
            if w == 1 and k != 1:
                self.z_out(m, h, z).start()

    def cross(self, m, h, k, w):
        @pl.when(self.at.w == w)
        def _():
            self.y_copy(m, h, self.at.order(k)).start()

    def finish(self, m):
        c0, n = self.columns[m]
        settle(self.full.at[0 : 8 * self.shard, pl.ds(c0, n)], self.recv.at[m, 9], self.at, False)

    def drain(self, ref):
        settle(ref.at[0 : 18 * self.shard, :], self.send.at[0], self.at, True)
        for w, blocks in ((0, 4), (1, 20)):

            @pl.when(self.at.w == w)
            def _(blocks=blocks):
                settle(ref.at[0 : blocks * self.shard, :], self.send.at[1], self.at, True)


class PairScatter:
    def __init__(self, at, full, shard, first, units, xs, xr, send, recv):
        self.at, self.full, self.shard, self.first = at, full, shard, first
        self.units, self.xs, self.xr, self.send, self.recv = units, xs, xr, send, recv
        self.base = {1: 0, 0: 11 if 1 in first else 9}

    def unit(self, m, z, y):
        ref, c0, n = self.full(m)
        size = 2 * self.shard
        return ref.at[pl.ds(pl.multiple_of((z * 2 + y) * size, size), size), pl.ds(c0, n)]

    def copy(self, m, src, dst, r, other):
        return pltpu.make_async_remote_copy(
            src_ref=src,
            dst_ref=dst,
            send_sem=self.send.at[0],
            recv_sem=self.recv.at[m, r],
            device_id=other,
            device_id_type=MESH,
        )

    def from_y(self, m, z):
        return self.units.at[self.base[m] + (10 if m in self.first else z)]

    def from_z(self, m, col, slot):
        return self.units.at[self.base[m] + (5 * col if m in self.first else 4) + slot]

    def column(self, col):
        return self.at.y if col == 0 else 1 - self.at.y

    def y_copy(self, m, z):
        return self.copy(m, self.unit(m, z, 1 - self.at.y), self.from_y(m, z), 10 if m in self.first else z, self.at.across_y())

    def z_copy(self, m, col, z, slot, other):
        return self.copy(
            m, self.unit(m, z, self.column(col)), self.from_z(m, col, slot), (5 * col if m in self.first else 4) + slot, other
        )

    def x_copy(self, m):
        return self.copy(m, self.xs.at[m], self.xr.at[m], 11, self.at.across_x())

    def begin(self, m, k):
        self.y_copy(m, self.at.order(k)).start()

    def pass_on(self, m, col, k, w):
        at = self.at
        z = at.order(k)
        if w == 0:
            self.z_copy(m, col, z, z, at.inward()).start()
        elif k == 1:
            self.z_copy(m, col, z, 4, at.outward()).start()
        else:
            self.z_copy(m, col, z, z if k == 3 else 4, at.inward()).start()

    def add_line(self, m, col, k, w, extra):
        at = self.at
        z = at.order(k)
        ref = self.unit(m, z, self.column(col))
        parts = list(extra)
        if k == 0:
            self.z_copy(m, col, z, 4, at.inward()).wait_recv()
            parts.append(self.from_z(m, col, 4))
        if w == 1:
            self.z_copy(m, col, z, z, at.inward()).wait_recv()
            parts.append(self.from_z(m, col, z))
        if parts:
            v = ref[...].astype(jnp.float32)
            for part in parts:
                v = v + part[...].astype(jnp.float32)
            ref[...] = v.astype(jnp.bfloat16)

    def finish(self, m, out, second):
        at = self.at
        size = self.shard
        full, c0, n = self.full(m)

        def total(x):
            rows = pl.ds(pl.multiple_of(at.chip(at.z, at.y, x) * size, size), size)
            v = full[rows, pl.ds(c0, n)].astype(jnp.float32)
            if second:
                v = v + self.from_y(m, at.z)[pl.ds(pl.multiple_of(x * size, size), size), :].astype(jnp.float32)
            return v

        self.xs[m] = total(1 - at.x).astype(jnp.bfloat16)
        self.x_copy(m).start()
        out(at.x, total(at.x))

    def line(self, m, k, w, out):
        at = self.at

        @pl.when(at.w == w)
        def _():
            z = at.order(k)
            self.y_copy(m, z).wait_recv()
            self.add_line(m, 0, k, w, [self.from_y(m, z)])
            if k > 0:
                self.pass_on(m, 0, k, w)
            else:
                self.finish(m, out, False)

    def line_first(self, m, col, k, w):
        @pl.when(self.at.w == w)
        def _():
            self.add_line(m, col, k, w, [])
            if k > 0:
                self.pass_on(m, col, k, w)
            elif col == 1:
                self.y_copy(m, self.at.z).start()

    def meet(self, m, out):
        self.y_copy(m, self.at.z).wait_recv()
        self.finish(m, out, True)

    def last(self, m, out):
        self.x_copy(m).wait_recv()
        out(1 - self.at.x, self.xr[m].astype(jnp.float32))

    def drain(self, ref):
        settle(ref, self.send.at[0], self.at, True)


QKV, OUT, UP, DOWN, COLS = 0, 1536, 2048, 3072, 4096
PIECES = ((0, 384), (384, 768), (768, 1152), (1152, 1536), (1536, 2048))
LINE_FIRST = ()
PLAN = (
    ((0, 3, 0, 1), (0, 0, 0, 1), (0, 2, 0, 1), (0, 3, 0, 0), (3, 1, 0, 0, 0), (0, 0, 0, 0), (0, 1, 0, 0), (0, 3, 1, 1), (3, 0, 0, 0, 1), (0, 3, 1, 0), (4, 1, 0, 0, 0), (0, 4, 0, 1), (0, 1, 0, 1), (0, 2, 0, 0), (0, 2, 1, 0), (3, 1, 0, 0, 1), (0, 0, 1, 1), (3, 0, 0, 0, 0), (4, 0, 0, 0, 1), (2, 0), (0, 0, 1, 0), (0, 0, 2, 1), (3, 0, 0, 1, 0), (4, 0, 0, 0, 0), (0, 1, 1, 1), (1, 2, 0), (0, 3, 2, 1), (0, 1, 2, 1), (3, 0, 1, 0, 0), (3, 0, 0, 1, 1), (1, 1, 0), (0, 4, 0, 0), (0, 4, 1, 0), (1, 0, 0), (0, 0, 2, 0), (0, 2, 1, 1), (0, 2, 2, 1), (0, 1, 1, 0), (0, 1, 2, 0), (0, 3, 2, 0), (0, 0, 3, 1), (0, 4, 1, 1), (2, 1), (3, 1, 0, 1, 1), (0, 0, 3, 0), (0, 2, 2, 0), (0, 1, 3, 1), (1, 0, 1), (3, 1, 0, 2, 1), (1, 3, 0), (1, 0, 2), (0, 3, 3, 1), (0, 1, 3, 0), (1, 0, 3), (0, 2, 3, 1), (3, 0, 0, 2, 1), (3, 1, 0, 3, 1), (1, 2, 1), (0, 2, 3, 0), (1, 3, 1),),
    ((1, 1, 1), (0, 4, 2, 1), (1, 1, 2),),
    ((1, 1, 3), (0, 4, 3, 1), (1, 2, 2), (3, 0, 1, 0, 1), (3, 1, 1, 0, 0), (3, 0, 0, 2, 0), (0, 3, 3, 0),),
    ((3, 1, 1, 0, 1), (1, 3, 2), (1, 2, 3), (3, 0, 1, 1, 1), (0, 4, 2, 0), (0, 4, 3, 0), (4, 0, 0, 1, 0), (4, 1, 0, 0, 1), (1, 3, 3),),
    (),
    ((4, 0, 1, 0, 1), (1, 4, 0), (1, 4, 1), (4, 0, 1, 0, 0), (1, 4, 2), (3, 0, 0, 3, 1),),
    ((4, 1, 1, 0, 1), (1, 4, 3),),
    ((3, 0, 1, 1, 0), (3, 1, 1, 1, 1), (5,), (4, 0, 1, 1, 1),),
    (),
    ((3, 0, 1, 2, 1), (4, 0, 0, 1, 1),),
    ((4, 0, 0, 2, 0),),
    (),
    ((3, 1, 0, 1, 0),),
    ((3, 0, 0, 3, 0), (3, 1, 1, 1, 0), (3, 0, 1, 3, 1),),
    (),
    (),
    ((3, 1, 1, 2, 1), (3, 0, 1, 2, 0), (4, 1, 0, 1, 0), (4, 0, 0, 2, 1), (4, 0, 1, 2, 1),),
    (),
    (),
    ((3, 1, 1, 3, 1), (4, 0, 0, 3, 1),),
    ((4, 0, 1, 3, 1), (4, 1, 0, 1, 1), (4, 1, 1, 1, 1), (4, 0, 1, 1, 0), (4, 0, 1, 2, 0), (3, 0, 1, 3, 0), (4, 0, 1, 3, 0), (3, 1, 0, 2, 0),),
    ((4, 1, 0, 2, 1),),
    ((4, 0, 0, 3, 0), (3, 1, 0, 3, 0), (3, 1, 1, 2, 0), (3, 1, 1, 3, 0),),
    (),
    (),
    ((4, 1, 0, 3, 1), (4, 1, 1, 0, 0), (4, 1, 1, 1, 0),),
    (),
    (),
    ((4, 1, 1, 2, 1), (4, 1, 0, 2, 0), (4, 1, 0, 3, 0), (4, 1, 1, 2, 0), (4, 1, 1, 3, 0), (4, 1, 1, 3, 1),),
    (),
    (),
    (),
    (),
    (),
    (),
    (),
    (),
    ((13, 1, 3), (13, 1, 2), (13, 1, 1), (13, 1, 0),),
    (),
    (),
    (),
    (),
    (),
    ((14, 1, 3, 0),),
    (),
    (),
    ((14, 1, 2, 0),),
    (),
    (),
    ((13, 0, 3),),
    ((14, 1, 3, 1),),
    ((13, 0, 2), (13, 0, 1),),
    (),
    (),
    (),
    (),
    (),
    (),
    (),
    (),
    (),
    (),
    (),
    ((14, 0, 3, 0),),
    (),
    (),
    ((10, 4, 3),),
    ((14, 1, 1, 0), (10, 0, 3),),
    (),
    ((14, 1, 2, 1), (14, 1, 1, 1), (14, 0, 2, 0), (10, 4, 2),),
    ((14, 0, 3, 1), (10, 4, 1), (10, 1, 3),),
    ((10, 4, 0),),
    ((11, 4, 3),),
    ((10, 2, 3), (10, 2, 2), (11, 4, 2), (10, 1, 2), (10, 1, 1), (14, 0, 1, 0),),
    ((10, 2, 1), (11, 1, 3), (12, 4, 3, 0), (10, 1, 0),),
    ((14, 1, 0, 0), (10, 0, 2), (11, 4, 1),),
    ((13, 0, 0), (11, 4, 0),),
    (),
    (),
    ((10, 2, 0), (11, 2, 3), (14, 1, 0, 1),),
    ((11, 0, 3),),
    ((14, 0, 2, 1), (11, 1, 2), (11, 2, 2),),
    ((10, 3, 3), (10, 3, 2), (10, 3, 1),),
    (),
    (),
    ((11, 1, 1), (12, 1, 3, 0), (10, 0, 1), (12, 4, 3, 1), (14, 0, 1, 1), (12, 4, 2, 0), (11, 0, 2), (12, 1, 2, 0), (11, 3, 3),),
    (),
    ((11, 2, 1), (12, 1, 3, 1), (12, 2, 3, 0), (11, 3, 2), (12, 2, 2, 0), (11, 3, 1), (12, 0, 3, 0), (12, 4, 2, 1), (12, 4, 1, 1),),
    (),
    ((10, 3, 0), (12, 1, 2, 1), (12, 3, 3, 0), (12, 2, 3, 1), (11, 2, 0), (12, 1, 1, 1), (12, 0, 2, 0), (10, 0, 0), (11, 1, 0), (12, 3, 2, 0),),
    (),
    ((12, 0, 3, 1), (11, 0, 1), (12, 4, 1, 0), (12, 3, 3, 1), (14, 0, 0, 0), (14, 0, 0, 1), (12, 2, 2, 1), (12, 2, 1, 0), (12, 2, 1, 1),),
    (),
    ((12, 3, 1, 0), (12, 1, 1, 0), (12, 3, 2, 1), (12, 3, 1, 1), (11, 3, 0), (11, 0, 0), (12, 0, 1, 0), (12, 0, 2, 1), (12, 0, 1, 1), (12, 1, 0, 0),),
    (),
    ((12, 4, 0, 1), (12, 2, 0, 0), (15, 0), (15, 1), (12, 1, 0, 1), (12, 4, 0, 0), (12, 3, 0, 0), (12, 2, 0, 1), (12, 3, 0, 1), (12, 0, 0, 1), (12, 0, 0, 0),),
)
BF, F32 = jnp.bfloat16, jnp.float32
SUMS = ("bq", "bv", "bout", "bdown", "g1", "s1", "g2", "s2", "x", "mid", "res", "branch", "feed")
BLOCK = 32


def nn(a, b):
    return lax.dot_general(a, b, (((1,), (0,)), ((), ())), preferred_element_type=F32)


def nt(a, b):
    return lax.dot_general(a, b, (((1,), (1,)), ((), ())), preferred_element_type=F32)


def tn(a, b):
    return lax.dot_general(a, b, (((0,), (0,)), ((), ())), preferred_element_type=F32)


def at_rows(start, size):
    return pl.ds(pl.multiple_of(start, size), size)


def fold(v):
    return jnp.sum(v.reshape(v.shape[0] // 8, 8, v.shape[1]), axis=0)


def normed(v):
    centre = jnp.mean(v, axis=1, keepdims=True)
    offset = v - centre
    r = lax.rsqrt(jnp.mean(offset * offset, axis=1, keepdims=True) + eps_norm)
    return offset * r, r


def norm_back(dy, n, r, gain):
    dn = dy * gain
    first = jnp.mean(dn, axis=1, keepdims=True)
    second = jnp.mean(dn * n, axis=1, keepdims=True)
    return r * (dn - first - n * second)


def block_kernel(
    counts, x_hbm, cot_hbm, wqkv, wout, wup, wdown, bqv, bout, bup, bdown, g1, s1, g2, s2,
    act_hbm, gin_hbm, qkv_hbm, out_hbm, up_hbm, down_hbm, o_sums,
    x_ref, cot_ref, act_out, gin_out, o_qkv, o_out, o_up, o_down,
    W, G2, G3, xh, yh, xf, yf, zl, units, xs2, xr2,
    rows1, dfeed, qkv, probs, heads, mid, rows2, act, gp, datt,
    own_a, own_c, send_t, send_x, got, got_t, acc, acc_up, sums, sums_got,
    sem_in, ag_send, ag_recv, pg_send, pg_recv, rs_send, rs_recv, ps_send, ps_recv,
    pair_send, pair_recv, sums_send, sums_recv,
):
    at = Place()
    greet(at)
    rows_in = [pltpu.make_async_copy(a, b, sem_in.at[1 + i]) for i, (a, b) in enumerate(((x_hbm, x_ref), (cot_hbm, cot_ref)))]
    for c in rows_in:
        c.start()
    t, x = at.t, at.x
    shard = wup.shape[0]
    own = x_ref.shape[0]
    width = x_ref.shape[1]
    dbr = dfeed.at[0 : 2 * own, :]
    dproj = qkv

    def spot(far_x, far_t):
        return at_rows((far_x * 2 + far_t) * own, own)

    mine, theirs = at_rows(t * own, own), at_rows((1 - t) * own, own)

    here = at_rows(at.dp * shard, shard)
    quarter = pl.ds(pl.multiple_of(x * 1024, 1024), 1024)
    loads = [
        pltpu.make_async_copy(src, W.at[here, pl.ds(c0, n)], sem_in.at[0])
        for src, c0, n in (
            [(wqkv.at[j, :, pl.ds(128 * h, 128)], QKV + 384 * h + 128 * j, 128) for h in range(4) for j in range(3)]
            + [(wout, OUT, 512), (wup.at[:, quarter], UP, 1024), (wdown.at[:, quarter], DOWN, 1024)]
        )
    ]
    for c in loads:
        c.start()
    enter(at)
    g = Gather(at, W, shard, PIECES, ag_send, ag_recv)
    pg = PairGather(at, W, shard, ((UP, 1024), (DOWN, 1024)), (wup, wdown), pg_send, pg_recv)
    pltpu.make_async_copy(W.at[here, :], W.at[here, :], sem_in.at[0]).wait()

    home = {0: (W, DOWN, DOWN + 384), 1: (W, DOWN + 384, DOWN + 768), 2: (G3, 512, 896), 3: (W, OUT, OUT + 384), 4: (G3, 0, 512)}
    sc = Scatter(at, lambda p: home[p], shard, PIECES, xh, yh, xf, yf, zl, rs_send, rs_recv)
    home_pair = {0: (W, UP, 1024), 1: (G2, 0, 1024)}
    ps = PairScatter(at, lambda m: home_pair[m], shard, LINE_FIRST, units, xs2, xr2, ps_send, ps_recv)

    def write(p):
        def store(total):
            if p < 4:
                for j in range(3):
                    o_qkv[j, :, 128 * p : 128 * (p + 1)] = total[:, 128 * j : 128 * (j + 1)]
            else:
                o_out[...] = total
        return store

    def write_pair(m):
        ref = o_up if m == 0 else o_down

        def store(far_x, total):
            ref[:, pl.ds(pl.multiple_of(far_x * 1024, 1024), 1024)] = total
        return store

    def share_feed():
        shares.append(share(2, dfeed, spot(x, t), at.across_x()))

    actions = {
        0: g.line, 1: g.plane, 2: lambda m: pg.x_copy(m).start(), 3: pg.line, 4: pg.cross, 5: share_feed,
        10: sc.begin, 11: sc.plane, 12: lambda p, k, w: sc.line(p, k, w, write(p)),
        13: ps.begin, 14: lambda m, k, w: ps.line(m, k, w, write_pair(m)), 15: lambda m: ps.last(m, write_pair(m)),
        16: ps.line_first, 17: lambda m: ps.meet(m, write_pair(m)),
    }
    done = [0]

    def run(part):
        while done[0] <= min(part, len(PLAN) - 1):
            for kind, *a in PLAN[done[0]]:
                actions[kind](*a)
            done[0] += 1

    def quiet(part):
        return part >= len(PLAN) or not PLAN[part]

    def send(i, src, dst, other):
        return pltpu.make_async_remote_copy(
            src_ref=src, dst_ref=dst, send_sem=pair_send.at[i], recv_sem=pair_recv.at[i],
            device_id=other, device_id_type=MESH,
        )

    def share(i, ref, r, other):
        c = send(i, ref.at[r, :], ref.at[r, :], other)
        c.start()
        return c

    def take(i, ref, r):
        send(i, ref.at[r, :], ref.at[r, :], at.twin()).wait_recv()

    for ref in (acc, acc_up):
        ref[...] = jnp.zeros_like(ref)
    total_of = {name: acc.at[i] for i, name in enumerate(SUMS)}

    def add(name, v):
        ref = total_of[name]
        ref[...] += fold(v)

    def valid_of(image, start, size):
        slot = lax.broadcasted_iota(jnp.int32, (size, 1), 0) + start
        return slot < counts[image] + BUFFER

    def each_block(body):
        def go(b, _):
            body(b * BLOCK, pl.ds(pl.multiple_of(b * BLOCK, BLOCK), BLOCK))
            return 0
        lax.fori_loop(0, own // BLOCK, go, 0)

    def tiles(first, last, body, size=256):
        def go(i, _):
            body(pl.multiple_of(i * size, size))
            return 0
        lax.fori_loop(first // size, last // size, go, 0)

    def first_norm(b, r):
        xv = x_ref[r, :].astype(F32)
        keep = valid_of(t, b, BLOCK).astype(F32)
        n, _ = normed(xv)
        mine_b = pl.ds(pl.multiple_of(t * own + b, BLOCK), BLOCK)
        rows1[mine_b, :] = (n * g1[...] + s1[...]).astype(BF)
        add("x", keep * xv * xv)
        low = (cot_ref[r, :].astype(F32) * keep).astype(BF)
        dfeed[pl.ds(pl.multiple_of((x * 2 + t) * own + b, BLOCK), BLOCK), :] = low
        add("bdown", low.astype(F32))

    for c in rows_in:
        c.wait()
    run(0)
    each_block(first_norm)
    shares = [share(0, rows1, mine, at.twin()), share(1, dfeed, spot(x, t), at.twin())]

    def project(j):
        heads_of = pl.ds(pl.multiple_of(t * 512 + 128 * j, 128), 128)
        cols = pl.ds(QKV + 384 * j, 384)
        bias = jnp.concatenate([bqv[0:1, heads_of], jnp.zeros((1, 128), F32), bqv[1:2, heads_of]], axis=1)
        scale = jnp.where(lax.broadcasted_iota(jnp.int32, (1, 384), 1) < 128, HD**-0.5, 1.0)

        def body(i, _):
            r = at_rows(i * own, own)
            qkv[r, pl.ds(384 * j, 384)] = ((nn(rows1[r, :], W[:, cols]) + bias) * scale).astype(BF)
            return 0
        lax.fori_loop(0, 2, body, 0)

    first_lanes = lax.broadcasted_iota(jnp.int32, (own, 128), 1) < HD

    def attend(image, j):
        r = pl.ds(pl.multiple_of(image * own, own), own)
        c = 384 * j
        q2 = qkv[r, c : c + 128]
        k2 = qkv[r, c + 128 : c + 256]
        v_t = qkv[r, c + 256 : c + 384].T
        hide = jnp.where(valid_of(image, 0, own), 0.0, -1e30)
        outs = []
        for a in range(2):
            qm = jnp.where(first_lanes if a == 0 else ~first_lanes, q2, jnp.zeros_like(q2))
            s = nt(k2, qm) + hide
            e = jnp.exp(s - jnp.max(s, axis=0, keepdims=True))
            low = (e * (1.0 / jnp.sum(e, axis=0, keepdims=True))).astype(BF)
            probs[(j * 2 + image) * 2 + a] = low
            outs.append(nn(v_t[a * HD : (a + 1) * HD], low))
        heads[r, 128 * j : 128 * (j + 1)] = jnp.concatenate(outs, axis=0).T.astype(BF)

    def images(part, body, j):
        run(part)
        if quiet(part + 1):
            def go(i, _):
                body(i, j)
                return 0
            lax.fori_loop(0, 2, go, 0)
        else:
            body(0, j)
            run(part + 1)
            body(1, j)

    for j in range(4):
        run(1 + 4 * j)
        g.finish(j)
        if j == 0:
            take(0, rows1, theirs)
        run(2 + 4 * j)
        project(j)
        images(3 + 4 * j, attend, j)
    run(17)
    g.finish(4)
    run(18)

    def others(i, src, cols, k):
        def body(c):
            send_t[0, :, pl.ds(c, 512)] = nt(src[theirs, :], W[pl.ds(c, 512), cols]).astype(BF)
        tiles(0, width, body, 512)
        copy = send(i, send_t.at[0], got.at[k], at.twin())
        copy.start()
        return copy

    def owns(src, cols, keep):
        def body(c):
            keep[:, pl.ds(c, 512)] = nt(src[mine, :], W[pl.ds(c, 512), cols])
        tiles(0, width, body, 512)

    branch_copy = others(3, heads, pl.ds(OUT, 512), 0)
    run(19)
    owns(heads, pl.ds(OUT, 512), own_a)
    run(20)
    branch_copy.wait()

    def second_norm(b, r):
        keep = valid_of(t, b, BLOCK).astype(F32)
        branch = own_a[r, :] + got[0, r, :].astype(F32) + bout[...]
        m = x_ref[r, :].astype(F32) + branch
        mid[r, :] = m
        add("branch", keep * branch * branch)
        add("mid", keep * m * m)
        n, _ = normed(m)
        rows2[pl.ds(pl.multiple_of((x * 2 + t) * own + b, BLOCK), BLOCK), :] = (n * g2[...] + s2[...]).astype(BF)

    run(21)
    each_block(second_norm)
    run(22)
    shares.append(share(4, rows2, spot(x, t), at.across_x()))
    shares.append(share(5, rows2, spot(x, t), at.twin()))
    run(23)

    take(2, dfeed, spot(1 - x, t))
    shares.append(share(6, dfeed, spot(1 - x, t), at.twin()))
    take(1, dfeed, spot(x, 1 - t))
    run(24)
    take(5, rows2, spot(x, 1 - t))

    chip_rows = lambda far_x: at_rows(far_x * 2 * own, 2 * own)

    def halves(part, body):
        run(part)
        if quiet(part + 1):
            tiles(0, 1024, body, 512)
        else:
            body(0)
            run(part + 1)
            body(512)

    def hidden(far_x, part):
        r = chip_rows(far_x)

        def body(c):
            def part_of(d):
                cols = pl.multiple_of(c + d, 256)
                lanes = pl.ds(pl.multiple_of(t * 2048 + x * 1024 + cols, 256), 256)
                u = nn(rows2[r, :], W[:, pl.ds(UP + cols, 256)]) + bup[:, lanes]
                below = 0.5 * (1.0 + lax.erf(u * (0.5**0.5)))
                dense = jnp.exp(-0.5 * u * u) * 0.3989422804014327
                act[r, pl.ds(cols, 256)] = (u * below).astype(BF)
                gp[r, pl.ds(cols, 256)] = (below + u * dense).astype(BF)
            tiles(0, 512, part_of)
        halves(part, body)

    def grad_down(c):
        def part(d):
            cols = pl.ds(pl.multiple_of(c + d, 256), 256)
            G2[:, cols] = tn(dfeed[...], act[:, cols]).astype(BF)
        tiles(0, 512, part)

    run(25)
    pg.finish(0)
    hidden(x, 26)
    run(28)
    take(4, rows2, spot(1 - x, t))
    shares.append(share(7, rows2, spot(1 - x, t), at.twin()))
    run(29)
    take(7, rows2, spot(1 - x, 1 - t))
    hidden(1 - x, 30)
    take(6, dfeed, spot(1 - x, 1 - t))
    halves(33, grad_down)
    run(37)

    def back_act(far_x):
        r = chip_rows(far_x)

        def body(c):
            cols = pl.ds(c, 256)
            d = nn(dfeed[r, :], W[:, pl.ds(DOWN + c, 256)])
            low = (d * gp[r, cols].astype(F32)).astype(BF)
            gp[r, cols] = low
            acc_up[t * 2 + x, :, cols] += fold(low.astype(F32))
        tiles(0, 1024, body)

    class Sum4:
        def __init__(self, i, n, src, cols, keep, parts):
            self.i, self.n, self.src, self.cols, self.keep, self.parts = i, n, src, cols, keep, parts

        def away(self, far_x, slot):
            r = spot(far_x, 1 - t)

            def body(c):
                send_t[slot, :, pl.ds(c, 512)] = nt(self.src[r, :], W[pl.ds(c, 512), self.cols]).astype(BF)
            tiles(0, width, body, 512)
            copy = send(self.i + slot, send_t.at[slot], got_t.at[self.n, slot], at.twin())
            copy.start()
            return copy

        def far(self):
            first = self.away(1 - x, 0)

            r = spot(1 - x, t)

            def product(c):
                send_x[self.n, :, pl.ds(c, 512)] = nt(self.src[r, :], W[pl.ds(c, 512), self.cols]).astype(BF)
            tiles(0, width, product, 512)
            run(self.parts[0])
            first.wait()

            def body(b, r):
                send_x[self.n, r, :] = send_x[self.n, r, :] + got_t[self.n, 0, r, :]
            each_block(body)
            self.cross = send(self.i + 2, send_x.at[self.n], got.at[2 + self.n], at.across_x())
            run(self.parts[1])
            self.cross.start()

        def near(self):
            self.second = self.away(x, 1)
            r = spot(x, t)

            def body(c):
                self.keep[:, pl.ds(c, 512)] = nt(self.src[r, :], W[pl.ds(c, 512), self.cols])
            tiles(0, width, body, 512)

        def value(self, r):
            return self.keep[r, :] + got_t[self.n, 1, r, :].astype(F32) + got[2 + self.n, r, :].astype(F32)

    pg.finish(1)
    run(39)
    back_act(1 - x)
    run(40)
    two = Sum4(8, 0, gp, pl.ds(UP, 1024), own_a, (41, 42))
    two.far()
    run(43)
    back_act(x)
    run(44)
    two.near()
    g.drain()
    pg.drain(dfeed)

    def grad_up(c):
        def part(d):
            cols = pl.multiple_of(c + d, 256)
            W[:, pl.ds(UP + cols, 256)] = tn(rows2[...], gp[:, pl.ds(cols, 256)]).astype(BF)
        tiles(0, 512, part)

    halves(45, grad_up)
    run(48)
    four = Sum4(11, 1, act, pl.ds(DOWN, 1024), own_c, (49, 50))
    four.far()
    run(51)
    two.second.wait()
    four.near()
    run(52)
    two.cross.wait()
    for i in (1, 2, 5):
        shares[i].wait_send()

    def second_back(b, r):
        dy = two.value(r)
        n, scale = normed(mid[r, :])
        keep = valid_of(t, b, BLOCK).astype(F32)
        add("g2", dy * n)
        add("s2", dy)
        d = cot_ref[r, :].astype(F32) * keep + norm_back(dy, n, scale, g2[...])
        gin_out[r, :] = d
        low = d.astype(BF)
        dbr[pl.ds(pl.multiple_of(t * own + b, BLOCK), BLOCK), :] = low
        add("bout", low.astype(F32))

    run(54)
    each_block(second_back)
    shares.append(share(14, dbr, mine, at.twin()))
    run(55)
    take(14, dbr, theirs)
    run(56)

    def back_heads(c):
        datt[:, pl.ds(c, 512)] = nn(dbr[...], W[:, pl.ds(OUT + c, 512)]).astype(BF)

    back_heads(0)
    run(59)

    def grad_out(c):
        G3[:, pl.ds(c, 512)] = tn(dbr[...], heads[:, pl.ds(c, 512)]).astype(BF)

    grad_out(0)
    run(60)

    def grad_heads(p):
        ref, c0, c1 = home[p]

        def body(c):
            ref[pl.ds(c, 512), c0:c1] = tn(rows1[:, pl.ds(c, 512)], dproj[:, 384 * p : 384 * (p + 1)]).astype(BF)
        tiles(0, width, body, 512)

    def attend_back(image, j):
        r = pl.ds(pl.multiple_of(image * own, own), own)
        c = 384 * j
        q2 = qkv[r, c : c + 128]
        k_t = qkv[r, c + 128 : c + 256].T
        v2 = qkv[r, c + 256 : c + 384]
        da = datt[r, 128 * j : 128 * (j + 1)]
        dq, dk, dv = [], [], []
        for a in range(2):
            dam = jnp.where(first_lanes if a == 0 else ~first_lanes, da, jnp.zeros_like(da))
            low = probs[(j * 2 + image) * 2 + a]
            p = low.astype(F32)
            dp = nt(v2, dam)
            ds = (p * (dp - jnp.sum(p * dp, axis=0, keepdims=True))).astype(BF)
            dq.append(nn(k_t[a * HD : (a + 1) * HD], ds))
            dk.append(nn(ds, q2))
            dv.append(nn(low, da))
        for base, v in (
            (0, jnp.concatenate(dq, axis=0).T * HD**-0.5),
            (128, jnp.where(first_lanes, dk[0], dk[1])),
            (256, jnp.where(first_lanes, dv[0], dv[1])),
        ):
            v = v.astype(BF)
            dproj[r, c + base : c + base + 128] = v
            if base != 128:
                lanes = pl.ds(pl.multiple_of(t * 512 + 128 * j, 128), 128)
                ref = total_of["bq" if base == 0 else "bv"]
                ref[:, lanes] += fold(v.astype(F32))

    def finish_feed(b, r):
        keep = valid_of(t, b, BLOCK).astype(F32)
        feed = four.value(r) + bdown[...]
        res = mid[r, :] + feed
        add("feed", keep * feed * feed)
        add("res", keep * res * res)
        act_out[r, :] = (keep * res).astype(BF)

    for j in range(3):
        images(61 + 4 * j, attend_back, j)
        run(63 + 4 * j)
        grad_heads(j)
    run(73)
    four.second.wait()
    four.cross.wait()
    run(74)
    each_block(finish_feed)
    outs = [pltpu.make_async_copy(act_out, act_hbm, sem_in.at[3])]
    outs[0].start()
    images(75, attend_back, 3)
    run(77)
    one_copy = others(15, dproj, pl.ds(QKV, 1536), 1)
    run(78)
    grad_heads(3)
    run(80)
    owns(dproj, pl.ds(QKV, 1536), own_a)
    run(81)
    one_copy.wait()
    run(82)

    def first_back(b, r):
        dy = own_a[r, :] + got[1, r, :].astype(F32)
        n, scale = normed(x_ref[r, :].astype(F32))
        add("g1", dy * n)
        add("s1", dy)
        gin_out[r, :] += norm_back(dy, n, scale, g1[...])

    each_block(first_back)
    outs.append(pltpu.make_async_copy(gin_out, gin_hbm, sem_in.at[4]))
    outs[1].start()
    run(83)

    for i in range(8):
        sums[i : i + 1, :] = jnp.sum(acc[i], axis=0, keepdims=True)
    for i in range(4):
        sums[8 + i : 9 + i, :] = jnp.sum(acc_up[i], axis=0, keepdims=True)
    lane = lax.broadcasted_iota(jnp.int32, (1, width), 1)
    row = jnp.where(lane == 5, (counts[t] + BUFFER).astype(F32), 0.0)
    for i, name in enumerate(("x", "mid", "res", "branch", "feed")):
        row = jnp.where(lane == i, jnp.sum(jnp.sum(total_of[name][...], axis=0, keepdims=True), axis=1, keepdims=True), row)
    sums[12:13, :] = row
    sums[13:16, :] = jnp.zeros((3, width), F32)
    for i, other in enumerate((at.twin(), at.across_x(), at.across_y(), at.near(), at.far())):
        c = pltpu.make_async_remote_copy(
            src_ref=sums, dst_ref=sums_got.at[i], send_sem=sums_send.at[i], recv_sem=sums_recv.at[i],
            device_id=other, device_id_type=MESH,
        )
        run(84 + 2 * i)
        c.start()
        run(85 + 2 * i)
        c.wait()
        sums[...] += sums_got[i]
    o_sums[...] = sums[...]
    run(1000)
    for i, (a, b) in enumerate(((o_qkv, qkv_hbm), (o_out, out_hbm), (o_up, up_hbm), (o_down, down_hbm))):
        outs.append(pltpu.make_async_copy(a, b, sem_in.at[5 + i]))
        outs[-1].start()
    sent = W.at[0 : 15 * shard, 0:2048]
    sc.drain(sent)
    ps.drain(sent)
    for c in outs:
        c.wait()
    for i in (0, 3, 4, 6, 7):
        shares[i].wait_send()


def block(counts, stream, cotangent, w_qkv, w_out_t, w_up, w_down_t, b_qv, b_out, b_up, b_down, g1, s1, g2, s2):
    own, width = stream.shape
    shard = w_up.shape[0]
    rows = 16 * shard
    group = 2 * own
    vmem = pl.BlockSpec(memory_space=pltpu.VMEM)
    hbm = pl.BlockSpec(memory_space=pl.ANY)
    dma = pltpu.SemaphoreType.DMA
    row = lambda v: v.reshape(1, -1)
    return pl.pallas_call(
        block_kernel,
        out_shape=(
            jax.ShapeDtypeStruct((own, width), BF),
            jax.ShapeDtypeStruct((own, width), F32),
            jax.ShapeDtypeStruct((3, shard, 512), F32),
            jax.ShapeDtypeStruct((shard, 512), F32),
            jax.ShapeDtypeStruct((shard, 2048), F32),
            jax.ShapeDtypeStruct((shard, 2048), F32),
            jax.ShapeDtypeStruct((16, width), F32),
        ),
        in_specs=[pl.BlockSpec(memory_space=pltpu.SMEM)] + [hbm] * 6 + [vmem] * 8,
        out_specs=(hbm,) * 6 + (vmem,),
        scratch_shapes=[
            pltpu.VMEM((own, width), BF),
            pltpu.VMEM((own, width), BF),
            pltpu.VMEM((own, width), BF),
            pltpu.VMEM((own, width), F32),
            pltpu.VMEM((3, shard, 512), F32),
            pltpu.VMEM((shard, 512), F32),
            pltpu.VMEM((shard, 2048), F32),
            pltpu.VMEM((shard, 2048), F32),
            pltpu.VMEM((rows, COLS), BF),
            pltpu.VMEM((rows, 1024), BF),
            pltpu.VMEM((rows, 1024), BF),
            pltpu.VMEM((4, shard // 2, 2048), BF),
            pltpu.VMEM((4, shard // 2, 2048), BF),
            pltpu.VMEM((4, shard, 2048), BF),
            pltpu.VMEM((4, shard, 2048), BF),
            pltpu.VMEM((5, shard, 2048), BF),
            pltpu.VMEM((18 + 2 * len(LINE_FIRST), 2 * shard, 1024), BF),
            pltpu.VMEM((2, shard, 1024), BF),
            pltpu.VMEM((2, shard, 1024), BF),
            pltpu.VMEM((group, width), BF),
            pltpu.VMEM((2 * group, width), BF),
            pltpu.VMEM((group, 1536), BF),
            pltpu.VMEM((16, own, own), BF),
            pltpu.VMEM((group, 512), BF),
            pltpu.VMEM((own, width), F32),
            pltpu.VMEM((2 * group, width), BF),
            pltpu.VMEM((2 * group, 1024), BF),
            pltpu.VMEM((2 * group, 1024), BF),
            pltpu.VMEM((group, 512), BF),
            pltpu.VMEM((own, width), F32),
            pltpu.VMEM((own, width), F32),
            pltpu.VMEM((2, own, width), BF),
            pltpu.VMEM((2, own, width), BF),
            pltpu.VMEM((4, own, width), BF),
            pltpu.VMEM((2, 2, own, width), BF),
            pltpu.VMEM((len(SUMS), 8, width), F32),
            pltpu.VMEM((4, 8, 1024), F32),
            pltpu.VMEM((16, width), F32),
            pltpu.VMEM((5, 16, width), F32),
            dma((9,)),
            dma((2,)),
            dma((5, 13)),
            dma((2,)),
            dma((2, 10)),
            dma((1,)),
            dma((5, 13)),
            dma((1,)),
            dma((2, 12)),
            dma((16,)),
            dma((16,)),
            dma((5,)),
            dma((5,)),
        ],
        compiler_params=pltpu.CompilerParams(
            collective_id=1, has_side_effects=True, vmem_limit_bytes=63 << 20
        ),
    )(
        counts, stream, cotangent, w_qkv, w_out_t, w_up, w_down_t,
        b_qv, row(b_out), row(b_up), row(b_down), row(g1), row(s1), row(g2), row(s2),
    )


def close_kernel(*refs):
    big, sums, out, small, held, sem = refs[:6], refs[6], refs[7:13], refs[13:22], refs[22:28], refs[28]
    loads = [pltpu.make_async_copy(a, h, sem.at[0, i]) for i, (a, h) in enumerate(zip(big, held))]
    copies = [pltpu.make_async_copy(h, b, sem.at[1, i]) for i, (h, b) in enumerate(zip(held, out))]
    for c in loads:
        c.start()
    place = lax.axis_index("dp") * 2 + lax.axis_index("tensor")
    width = sums.shape[1]
    turned = pltpu.roll(sums[0:8, :], width - place * 32, 1)
    small[0][...] = turned[0:2, :32]
    for i in range(1, 7):
        small[i][...] = turned[i + 1 : i + 2, :32]
    up = pl.ds(pl.multiple_of((place % 8) * 128, 128), 128)
    which = lax.broadcasted_iota(jnp.int32, (8, 128), 0) == place // 8
    small[7][...] = jnp.sum(jnp.where(which, sums[8:16, up], 0.0), axis=0, keepdims=True)
    row = sums[12:13, :]
    small[8][...] = jnp.sqrt(row[:, 0:5] / (row[:, 5:6] * width))
    for load, c in zip(loads, copies):
        load.wait()
        c.start()
    for c in copies:
        c.wait()


def close(*arrays):
    vmem = pl.BlockSpec(memory_space=pltpu.VMEM)
    hbm = pl.BlockSpec(memory_space=pl.ANY)
    small = [(2, 32)] + [(1, 32)] * 6 + [(1, 128), (1, 5)]
    return pl.pallas_call(
        close_kernel,
        out_shape=tuple(jax.ShapeDtypeStruct(a.shape, a.dtype) for a in arrays[:6])
        + tuple(jax.ShapeDtypeStruct(n, F32) for n in small),
        in_specs=[hbm] * 6 + [vmem],
        out_specs=(hbm,) * 6 + (vmem,) * 9,
        scratch_shapes=[pltpu.VMEM(a.shape, a.dtype) for a in arrays[:6]] + [pltpu.SemaphoreType.DMA((2, 6))],
    )(*arrays)


def local_fast(
    stream, counts, cotangent, w_qkv, b_qv, w_out, b_out, w_fc1, b_fc1, w_fc2, b_fc2,
    gain_one, shift_one, gain_two, shift_two,
):
    acts, grad_in, p_qkv, p_out, p_up, p_down, bqv, *rest = close(
        *block(
            counts, stream, cotangent, w_qkv, w_out.T, w_fc1, w_fc2.T, b_qv, b_out, b_fc1, b_fc2,
            gain_one, shift_one, gain_two, shift_two,
        )
    )
    bout, bdown, gain1, shift1, gain2, shift2, bup, rms = (v.reshape(-1) for v in rest[:8])
    return (
        acts, grad_in, p_qkv, bqv, p_out.T, bout, p_up, bup, p_down.T, bdown,
        gain1, shift1, gain2, shift2, rms,
    )

def layer_norm(values, gain, shift):
    centre = jnp.mean(values, axis=-1, keepdims=True)
    offset = values - centre
    spread = jnp.mean(offset * offset, axis=-1, keepdims=True)
    return offset * lax.rsqrt(spread + eps_norm) * gain + shift


def gelu_exact(values):
    return jax.nn.gelu(values, approximate=False)


def masked_scores(queries, key_rows, validity):
    scores = jnp.einsum(
        "bqhd,bkhd->bhqk", queries, key_rows, preferred_element_type=jnp.float32
    ) * HD ** (-0.5)
    return jnp.where(validity[:, None, None, :] > 0, scores, -1e30)


def attend_block(members):
    queries, key_rows, values, validity = members
    scores = masked_scores(queries, key_rows, validity)
    highest = jnp.max(scores, axis=-1, keepdims=True)
    expo_terms = jnp.exp(scores - highest)
    totals = jnp.sum(expo_terms, axis=-1, keepdims=True)
    weights = (expo_terms / totals).astype(jnp.bfloat16)
    mixture = jnp.einsum("bhqk,bkhd->bqhd", weights, values, preferred_element_type=jnp.float32)
    return (mixture.astype(jnp.bfloat16), (highest + jnp.log(totals))[..., 0])


def attend_back(members):
    queries, key_rows, values, validity, log_total, d_mixture = members
    scores = masked_scores(queries, key_rows, validity)
    probs = jnp.exp(scores - log_total[..., None])
    d_values = jnp.einsum(
        "bhqk,bqhd->bkhd", probs.astype(jnp.bfloat16), d_mixture, preferred_element_type=jnp.float32
    )
    d_probs = jnp.einsum("bqhd,bkhd->bhqk", d_mixture, values, preferred_element_type=jnp.float32)
    d_scores = (probs * (d_probs - jnp.sum(probs * d_probs, axis=-1, keepdims=True))).astype(
        jnp.bfloat16
    )
    d_queries = jnp.einsum(
        "bhqk,bkhd->bqhd", d_scores, key_rows, preferred_element_type=jnp.float32
    ) * HD ** (-0.5)
    d_keys = jnp.einsum(
        "bhqk,bqhd->bkhd", d_scores, queries, preferred_element_type=jnp.float32
    ) * HD ** (-0.5)
    return (
        d_queries.astype(jnp.bfloat16),
        d_keys.astype(jnp.bfloat16),
        d_values.astype(jnp.bfloat16),
    )


def local(
    stream,
    counts,
    cotangent,
    w_qkv,
    b_qv,
    w_out,
    b_out,
    w_fc1,
    b_fc1,
    w_fc2,
    b_fc2,
    gain_one,
    shift_one,
    gain_two,
    shift_two,
):
    tensor_pos = lax.axis_index("tensor")
    own_rows = stream.shape[0]
    width = stream.shape[1]
    own_images = own_rows // SLOTS
    slot_index = jnp.arange(SLOTS, dtype=jnp.int32)
    validity_all = (slot_index[None, :] < (BUFFER + counts)[:, None]).astype(jnp.float32)
    own_validity = lax.dynamic_slice_in_dim(validity_all, tensor_pos * own_images, own_images, 0)
    own_valid = own_validity.reshape(own_rows, 1)
    qkv_full, out_full, up_full, down_full = (
        lax.all_gather(w_qkv, "dp", axis=1, tiled=True),
        lax.all_gather(w_out, "dp", axis=1, tiled=True),
        lax.all_gather(w_fc1[None], "dp", axis=1, tiled=True),
        lax.all_gather(w_fc2, "dp", axis=1, tiled=True),
    )
    head_width = w_qkv.shape[2]
    unit_width = w_fc1.shape[1]
    bias_query = lax.dynamic_slice_in_dim(b_qv[0], tensor_pos * head_width, head_width, 0)
    bias_value = lax.dynamic_slice_in_dim(b_qv[1], tensor_pos * head_width, head_width, 0)
    bias_up = lax.dynamic_slice_in_dim(b_fc1, tensor_pos * unit_width, unit_width, 0)
    up_full = up_full[0]
    group_images = validity_all.shape[0]
    group_rows = group_images * SLOTS
    local_heads = head_width // HD
    pairing = 2
    block_count = group_images // pairing
    blocked_valid = validity_all.reshape(block_count, pairing, SLOTS)
    stream_f = stream.astype(jnp.float32)
    normed_one = layer_norm(stream_f, gain_one, shift_one).astype(jnp.bfloat16)
    first_rows = lax.all_gather(normed_one, "tensor", axis=0, tiled=True)
    projected = jnp.einsum("rd,cde->rce", first_rows, qkv_full, preferred_element_type=jnp.float32)
    shape_heads = (block_count, pairing, SLOTS, local_heads, HD)
    queries = (projected[:, 0] + bias_query).astype(jnp.bfloat16).reshape(shape_heads)
    key_rows = projected[:, 1].astype(jnp.bfloat16).reshape(shape_heads)
    values = (projected[:, 2] + bias_value).astype(jnp.bfloat16).reshape(shape_heads)
    mixture, log_total = lax.map(attend_block, (queries, key_rows, values, blocked_valid))
    attn_heads = mixture.reshape(group_rows, head_width)
    taken = attn_heads
    attn_total = lax.psum_scatter(
        jnp.dot(taken, out_full, preferred_element_type=jnp.float32).astype(jnp.bfloat16),
        "tensor",
        scatter_dimension=0,
        tiled=True,
    ).astype(jnp.float32)
    branch = attn_total + b_out
    middle = stream_f + branch
    normed_two = layer_norm(middle, gain_two, shift_two).astype(jnp.bfloat16)
    second_rows = lax.all_gather(normed_two, "tensor", axis=0, tiled=True)
    hidden_pre = jnp.dot(second_rows, up_full, preferred_element_type=jnp.float32) + bias_up
    hidden_act = gelu_exact(hidden_pre).astype(jnp.bfloat16)
    taken = hidden_act
    mlp_total = lax.psum_scatter(
        jnp.dot(taken, down_full, preferred_element_type=jnp.float32).astype(jnp.bfloat16),
        "tensor",
        scatter_dimension=0,
        tiled=True,
    ).astype(jnp.float32)
    feed = mlp_total + b_fc2
    result = middle + feed
    activations = (result * own_valid).astype(jnp.bfloat16)
    squares = jnp.stack(
        [
            jnp.sum(own_valid * member * member)
            for member in (stream_f, middle, result, branch, feed)
        ]
    )
    square_sums, valid_count = lax.psum((squares, jnp.sum(own_valid)), ("dp", "tensor"))
    rms_stats = jnp.sqrt(square_sums / (valid_count * width))
    d_result = cotangent.astype(jnp.float32) * own_valid
    d_feed_low = d_result.astype(jnp.bfloat16)
    d_feed_rows = lax.all_gather(d_feed_low, "tensor", axis=0, tiled=True)
    d_act = jnp.einsum("rd,ud->ru", d_feed_rows, down_full, preferred_element_type=jnp.float32)
    unused_act, gelu_pullback = jax.vjp(gelu_exact, hidden_pre)
    d_pre = gelu_pullback(d_act)[0].astype(jnp.bfloat16)
    grad_down = jnp.einsum("ru,rd->ud", hidden_act, d_feed_rows, preferred_element_type=jnp.float32)
    grad_up = jnp.einsum("rd,ru->du", second_rows, d_pre, preferred_element_type=jnp.float32)
    grad_bias_up = jnp.sum(d_pre, axis=0, dtype=jnp.float32)
    grad_bias_down = jnp.sum(d_feed_low, axis=0, dtype=jnp.float32)
    taken = d_pre
    d_normed_two = lax.psum_scatter(
        jnp.einsum("ru,du->rd", taken, up_full, preferred_element_type=jnp.float32).astype(
            jnp.bfloat16
        ),
        "tensor",
        scatter_dimension=0,
        tiled=True,
    ).astype(jnp.float32)
    unused_two, norm_two_pullback = jax.vjp(layer_norm, middle, gain_two, shift_two)
    d_middle_norm, grad_gain_two, grad_shift_two = norm_two_pullback(d_normed_two)
    d_middle = d_result + d_middle_norm
    d_branch_low = d_middle.astype(jnp.bfloat16)
    grad_bias_out = jnp.sum(d_branch_low, axis=0, dtype=jnp.float32)
    d_branch_rows = lax.all_gather(d_branch_low, "tensor", axis=0, tiled=True)
    d_attn = jnp.einsum(
        "rd,hd->rh", d_branch_rows, out_full, preferred_element_type=jnp.float32
    ).astype(jnp.bfloat16)
    grad_out = jnp.einsum(
        "rh,rd->hd", attn_heads, d_branch_rows, preferred_element_type=jnp.float32
    )
    d_queries, d_keys, d_values = lax.map(
        attend_back,
        (queries, key_rows, values, blocked_valid, log_total, d_attn.reshape(shape_heads)),
    )
    d_projected = jnp.stack(
        [
            d_queries.reshape(group_rows, head_width),
            d_keys.reshape(group_rows, head_width),
            d_values.reshape(group_rows, head_width),
        ],
        axis=1,
    )
    grad_qkv = jnp.einsum(
        "rd,rce->cde", first_rows, d_projected, preferred_element_type=jnp.float32
    )
    bias_terms = jnp.sum(d_projected, axis=0, dtype=jnp.float32)
    taken = d_projected
    d_normed_one = lax.psum_scatter(
        jnp.einsum("rce,cde->rd", taken, qkv_full, preferred_element_type=jnp.float32).astype(
            jnp.bfloat16
        ),
        "tensor",
        scatter_dimension=0,
        tiled=True,
    ).astype(jnp.float32)
    unused_one, norm_one_pullback = jax.vjp(layer_norm, stream_f, gain_one, shift_one)
    d_stream_norm, grad_gain_one, grad_shift_one = norm_one_pullback(d_normed_one)
    grad_input = d_middle + d_stream_norm
    grad_up = grad_up[None]
    bias_qv_full = lax.dynamic_update_slice(
        jnp.zeros((2, width), jnp.float32),
        jnp.stack([bias_terms[0], bias_terms[2]]),
        (jnp.int32(0), tensor_pos * head_width),
    )
    bias_up_full = lax.dynamic_update_slice(
        jnp.zeros((b_fc1.shape[0],), jnp.float32), grad_bias_up, (tensor_pos * unit_width,)
    )
    qkv_part, out_part, up_part, down_part = (
        lax.psum_scatter(
            grad_qkv.astype(jnp.bfloat16), "dp", scatter_dimension=1, tiled=True
        ).astype(jnp.float32),
        lax.psum_scatter(
            grad_out.astype(jnp.bfloat16), "dp", scatter_dimension=1, tiled=True
        ).astype(jnp.float32),
        lax.psum_scatter(
            grad_up.astype(jnp.bfloat16), "dp", scatter_dimension=1, tiled=True
        ).astype(jnp.float32),
        lax.psum_scatter(
            grad_down.astype(jnp.bfloat16), "dp", scatter_dimension=1, tiled=True
        ).astype(jnp.float32),
    )
    small_parts = (
        lax.psum_scatter(bias_qv_full, ("dp", "tensor"), scatter_dimension=1, tiled=True),
        lax.psum_scatter(grad_bias_out, ("dp", "tensor"), scatter_dimension=0, tiled=True),
        lax.psum_scatter(bias_up_full, ("dp", "tensor"), scatter_dimension=0, tiled=True),
        lax.psum_scatter(grad_bias_down, ("dp", "tensor"), scatter_dimension=0, tiled=True),
        lax.psum_scatter(grad_gain_one, ("dp", "tensor"), scatter_dimension=0, tiled=True),
        lax.psum_scatter(grad_shift_one, ("dp", "tensor"), scatter_dimension=0, tiled=True),
        lax.psum_scatter(grad_gain_two, ("dp", "tensor"), scatter_dimension=0, tiled=True),
        lax.psum_scatter(grad_shift_two, ("dp", "tensor"), scatter_dimension=0, tiled=True),
    )
    return (
        activations,
        grad_input,
        qkv_part,
        small_parts[0],
        out_part,
        small_parts[1],
        up_part[0],
        small_parts[2],
        down_part,
        small_parts[3],
        small_parts[4],
        small_parts[5],
        small_parts[6],
        small_parts[7],
        rms_stats,
    )


def solution(mesh):
    fast = mesh.shape["dp"] == 16 and mesh.shape["tensor"] == 2
    return jax.shard_map(
        local_fast if fast else local,
        mesh=mesh,
        in_specs=(
            P(("dp", "tensor"), None),
            P("dp"),
            P(("dp", "tensor"), None),
            P(None, "dp", "tensor"),
            P(),
            P("tensor", "dp"),
            P(),
            P("dp", "tensor"),
            P(),
            P("tensor", "dp"),
            P(),
            P(),
            P(),
            P(),
            P(),
        ),
        out_specs=(
            P(("dp", "tensor"), None),
            P(("dp", "tensor"), None),
            P(None, "dp", "tensor"),
            P(None, ("dp", "tensor")),
            P("tensor", "dp"),
            P(("dp", "tensor")),
            P("dp", "tensor"),
            P(("dp", "tensor")),
            P("tensor", "dp"),
            P(("dp", "tensor")),
            P(("dp", "tensor")),
            P(("dp", "tensor")),
            P(("dp", "tensor")),
            P(("dp", "tensor")),
            P(),
        ),
        check_vma=False,
    )
```

profile of v0, /device:TPU:0, one launch (start us, length us, event | category | flops | bytes accessed | tf_op | source)
XLA Modules:
  0.0 179.8 jit_solution(2584406283609722556)
XLA Ops:
  0.7 174.3 %shard_map.262 = (bf16[320,1024]{1,0:T(8,128)(2,1)}, f32[320,1024]{1,0:T(8,128)}, f32[3,64,512]{2,1,0:T(8,128)}, f32[64,512]{1,0:T(8,128)}, f32[64,2048]{1,0:T(8...) custom-call(s32[2]{0:T(128)} %counts.1, bf16[320,1024]{1,0:T(8,128)(2,1)} %x_hbm.1, bf16[320,1024]{1,0:T(8,128)(2,1)} %cot_hbm.1, ...), custom_call_target="tpu_custom_call" | custom-call | tf_op jit(solution)/shard_map/pallas_call | solution.py:1138
  175.0 4.6 %shard_map.263 = (bf16[320,1024]{1,0:T(8,128)(2,1)}, f32[320,1024]{1,0:T(8,128)}, f32[3,64,512]{2,1,0:T(8,128)}, f32[64,512]{1,0:T(8,128)}, f32[64,2048]{1,0:T(8...) custom-call(bf16[320,1024]{1,0:T(8,128)(2,1)} %get-tuple-element.37., ...), custom_call_target="tpu_custom_call" | custom-call | tf_op jit(solution)/shard_map/pallas_call | solution.py:1242
where the time goes:
time: 180 us
  Pallas kernels  179 us (99%)
    pallas_call x1, Pallas kernels, block(): pl.pallas_call(block_kernel, out_shape=(jax.ShapeDtypeStruct((own, width)...  174 us
    pallas_call x1, Pallas kernels, close(): pl.pallas_call(close_kernel, out_shape=tuple((jax.ShapeDtypeStruct(a.shap...  4.64 us

commit v1 on v0

--- a/solution.py
+++ b/solution.py
@@ -282,7 +282,8 @@
 
 
 class PairGather:
-    def __init__(self, at, full, shard, columns, sources, send, recv):
+    def __init__(self, at, full, shard, first, columns, sources, send, recv):
+        self.first = first
         self.at, self.full, self.shard, self.columns, self.sources = at, full, shard, columns, sources
         self.send, self.recv = send, recv
 
@@ -308,7 +309,7 @@
         at = self.at
         c0, n = self.columns[m]
         src = self.sources[m].at[:, pl.ds(pl.multiple_of((1 - at.x) * n, n), n)]
-        return self.copy(m, src, self.rows(m, at.z, at.y, at.x), 0, 8, at.across_x())
+        return self.copy(m, src, self.rows(m, at.z, at.y, at.x), 0, 16, at.across_x())
 
     def z_in(self, m, h, z):
         ref = self.rows(m, z, self.at.y, self.far_x(h))
@@ -320,7 +321,7 @@
 
     def y_copy(self, m, h, z):
         ref = self.rows(m, z, self.at.y, self.far_x(h))
-        return self.copy(m, ref, ref, 0, 9, self.at.across_y())
+        return self.copy(m, ref, ref, 0, 17, self.at.across_y())
 
     def line(self, m, h, k, w):
         at = self.at
@@ -332,7 +333,7 @@
             if k > 0:
                 settle(ref, self.recv.at[m, 4 * h + z], at, False)
             elif h == 1:
-                settle(ref, self.recv.at[m, 8], at, False)
+                settle(ref, self.recv.at[m, 16], at, False)
             if k == 0 or (k == 1 and w == 1):
                 self.z_in(m, h, z).start()
             if w == 1 and k != 1:
@@ -343,17 +344,47 @@
         def _():
             self.y_copy(m, h, self.at.order(k)).start()
 
+    def over_copy(self, m, h):
+        at = self.at
+        ref = self.rows(m, at.z, at.y, self.far_x(h))
+        return self.copy(m, ref, ref, 0, 17 + h, at.across_y())
+
+    def over(self, m, h):
+        at = self.at
+        if h == 1:
+            settle(self.rows(m, at.z, at.y, 1 - at.x), self.recv.at[m, 16], at, False)
+        self.over_copy(m, h).start()
+
+    def column_line(self, m, h, col, k, w):
+        at = self.at
+
+        @pl.when(at.w == w)
+        def _():
+            z = at.order(k)
+            ref = self.rows(m, z, at.y if col == 0 else 1 - at.y, self.far_x(h))
+            slot = 4 * (2 * h + col) + z
+            if k > 0:
+                settle(ref, self.recv.at[m, slot], at, False)
+            elif col == 1:
+                settle(ref, self.recv.at[m, 17 + h], at, False)
+            if k == 0 or (k == 1 and w == 1):
+                self.copy(m, ref, ref, 1, slot, at.inward()).start()
+            if w == 1 and k != 1:
+                self.copy(m, ref, ref, 1, slot, at.outward()).start()
+
     def finish(self, m):
-        c0, n = self.columns[m]
-        settle(self.full.at[0 : 8 * self.shard, pl.ds(c0, n)], self.recv.at[m, 9], self.at, False)
+        if m not in self.first:
+            c0, n = self.columns[m]
+            settle(self.full.at[0 : 8 * self.shard, pl.ds(c0, n)], self.recv.at[m, 17], self.at, False)
 
     def drain(self, ref):
-        settle(ref.at[0 : 18 * self.shard, :], self.send.at[0], self.at, True)
-        for w, blocks in ((0, 4), (1, 20)):
+        later = len(self.first)
+        settle(ref.at[0 : (18 - 6 * later) * self.shard // 2, :], self.send.at[0], self.at, True)
+        for w, blocks in ((0, 2), (1, 10)):
 
             @pl.when(self.at.w == w)
-            def _(blocks=blocks):
-                settle(ref.at[0 : blocks * self.shard, :], self.send.at[1], self.at, True)
+            def _(blocks=blocks * (2 + later)):
+                settle(ref.at[0 : blocks * self.shard // 2, :], self.send.at[1], self.at, True)
 
 
 class PairScatter:
@@ -480,103 +511,104 @@
 QKV, OUT, UP, DOWN, COLS = 0, 1536, 2048, 3072, 4096
 PIECES = ((0, 384), (384, 768), (768, 1152), (1152, 1536), (1536, 2048))
 LINE_FIRST = ()
+OVER_FIRST = (1,)
 PLAN = (
-    ((0, 3, 0, 1), (0, 0, 0, 1), (0, 2, 0, 1), (0, 3, 0, 0), (3, 1, 0, 0, 0), (0, 0, 0, 0), (0, 1, 0, 0), (0, 3, 1, 1), (3, 0, 0, 0, 1), (0, 3, 1, 0), (4, 1, 0, 0, 0), (0, 4, 0, 1), (0, 1, 0, 1), (0, 2, 0, 0), (0, 2, 1, 0), (3, 1, 0, 0, 1), (0, 0, 1, 1), (3, 0, 0, 0, 0), (4, 0, 0, 0, 1), (2, 0), (0, 0, 1, 0), (0, 0, 2, 1), (3, 0, 0, 1, 0), (4, 0, 0, 0, 0), (0, 1, 1, 1), (1, 2, 0), (0, 3, 2, 1), (0, 1, 2, 1), (3, 0, 1, 0, 0), (3, 0, 0, 1, 1), (1, 1, 0), (0, 4, 0, 0), (0, 4, 1, 0), (1, 0, 0), (0, 0, 2, 0), (0, 2, 1, 1), (0, 2, 2, 1), (0, 1, 1, 0), (0, 1, 2, 0), (0, 3, 2, 0), (0, 0, 3, 1), (0, 4, 1, 1), (2, 1), (3, 1, 0, 1, 1), (0, 0, 3, 0), (0, 2, 2, 0), (0, 1, 3, 1), (1, 0, 1), (3, 1, 0, 2, 1), (1, 3, 0), (1, 0, 2), (0, 3, 3, 1), (0, 1, 3, 0), (1, 0, 3), (0, 2, 3, 1), (3, 0, 0, 2, 1), (3, 1, 0, 3, 1), (1, 2, 1), (0, 2, 3, 0), (1, 3, 1),),
-    ((1, 1, 1), (0, 4, 2, 1), (1, 1, 2),),
-    ((1, 1, 3), (0, 4, 3, 1), (1, 2, 2), (3, 0, 1, 0, 1), (3, 1, 1, 0, 0), (3, 0, 0, 2, 0), (0, 3, 3, 0),),
-    ((3, 1, 1, 0, 1), (1, 3, 2), (1, 2, 3), (3, 0, 1, 1, 1), (0, 4, 2, 0), (0, 4, 3, 0), (4, 0, 0, 1, 0), (4, 1, 0, 0, 1), (1, 3, 3),),
-    (),
-    ((4, 0, 1, 0, 1), (1, 4, 0), (1, 4, 1), (4, 0, 1, 0, 0), (1, 4, 2), (3, 0, 0, 3, 1),),
-    ((4, 1, 1, 0, 1), (1, 4, 3),),
-    ((3, 0, 1, 1, 0), (3, 1, 1, 1, 1), (5,), (4, 0, 1, 1, 1),),
-    (),
-    ((3, 0, 1, 2, 1), (4, 0, 0, 1, 1),),
+    ((2, 1), (0, 0, 0, 1), (0, 0, 0, 0), (0, 3, 0, 1), (0, 2, 0, 0), (3, 0, 0, 0, 0), (0, 0, 1, 0), (0, 2, 0, 1), (6, 1, 0), (2, 0), (0, 1, 0, 1), (0, 1, 0, 0), (0, 3, 0, 0), (3, 0, 0, 0, 1), (0, 2, 1, 1), (0, 2, 1, 0), (0, 0, 1, 1), (0, 2, 2, 1), (0, 0, 2, 1), (0, 4, 0, 1), (0, 4, 0, 0), (6, 1, 1), (0, 0, 3, 1), (0, 3, 1, 1), (1, 0, 0), (0, 4, 1, 0), (3, 0, 1, 0, 0), (0, 3, 1, 0), (7, 1, 1, 1, 0, 0), (0, 0, 2, 0), (0, 1, 1, 1), (3, 0, 1, 0, 1), (0, 2, 3, 1), (0, 4, 1, 1), (1, 0, 1), (0, 1, 2, 1), (0, 0, 3, 0), (0, 1, 1, 0), (1, 2, 0), (0, 1, 2, 0), (1, 0, 2), (3, 0, 0, 1, 1), (0, 2, 2, 0), (0, 3, 2, 1), (0, 3, 3, 1), (0, 1, 3, 0), (1, 4, 0), (0, 1, 3, 1), (1, 0, 3), (3, 0, 1, 1, 0), (7, 1, 1, 1, 0, 1), (0, 4, 2, 1), (3, 0, 1, 1, 1), (7, 1, 1, 0, 0, 0), (1, 1, 0), (1, 3, 0), (7, 1, 1, 1, 1, 1),),
+    ((0, 3, 2, 0), (1, 2, 1), (7, 1, 0, 0, 0, 0), (0, 4, 3, 1), (7, 1, 1, 0, 0, 1), (0, 2, 3, 0), (0, 3, 3, 0), (3, 0, 0, 2, 1), (3, 0, 0, 3, 1), (1, 1, 1), (0, 4, 2, 0), (3, 0, 0, 1, 0), (0, 4, 3, 0), (3, 0, 1, 2, 1),),
+    ((1, 1, 2), (1, 1, 3), (7, 1, 0, 1, 0, 1), (3, 0, 0, 2, 0), (7, 1, 1, 0, 1, 1), (1, 2, 2), (1, 2, 3), (7, 1, 0, 0, 0, 1), (7, 1, 1, 0, 2, 1), (1, 4, 1),),
+    ((1, 3, 1), (1, 3, 2),),
+    (),
+    ((1, 4, 2), (4, 0, 1, 0, 0), (4, 0, 0, 0, 1), (1, 4, 3), (1, 3, 3), (7, 1, 0, 1, 0, 0),),
+    ((5,),),
+    ((7, 1, 1, 0, 1, 0), (4, 0, 0, 0, 0), (7, 1, 1, 1, 1, 0), (3, 0, 1, 2, 0), (4, 0, 0, 1, 0), (3, 0, 1, 3, 1), (4, 0, 1, 0, 1), (7, 1, 0, 0, 1, 1),),
+    (),
+    (),
     ((4, 0, 0, 2, 0),),
-    (),
-    ((3, 1, 0, 1, 0),),
-    ((3, 0, 0, 3, 0), (3, 1, 1, 1, 0), (3, 0, 1, 3, 1),),
-    (),
-    (),
-    ((3, 1, 1, 2, 1), (3, 0, 1, 2, 0), (4, 1, 0, 1, 0), (4, 0, 0, 2, 1), (4, 0, 1, 2, 1),),
-    (),
-    (),
-    ((3, 1, 1, 3, 1), (4, 0, 0, 3, 1),),
-    ((4, 0, 1, 3, 1), (4, 1, 0, 1, 1), (4, 1, 1, 1, 1), (4, 0, 1, 1, 0), (4, 0, 1, 2, 0), (3, 0, 1, 3, 0), (4, 0, 1, 3, 0), (3, 1, 0, 2, 0),),
-    ((4, 1, 0, 2, 1),),
-    ((4, 0, 0, 3, 0), (3, 1, 0, 3, 0), (3, 1, 1, 2, 0), (3, 1, 1, 3, 0),),
-    (),
-    (),
-    ((4, 1, 0, 3, 1), (4, 1, 1, 0, 0), (4, 1, 1, 1, 0),),
-    (),
-    (),
-    ((4, 1, 1, 2, 1), (4, 1, 0, 2, 0), (4, 1, 0, 3, 0), (4, 1, 1, 2, 0), (4, 1, 1, 3, 0), (4, 1, 1, 3, 1),),
-    (),
-    (),
-    (),
-    (),
-    (),
-    (),
-    (),
-    (),
-    ((13, 1, 3), (13, 1, 2), (13, 1, 1), (13, 1, 0),),
-    (),
-    (),
-    (),
-    (),
-    (),
-    ((14, 1, 3, 0),),
-    (),
-    (),
+    ((7, 1, 0, 1, 1, 0),),
+    (),
+    ((7, 1, 0, 1, 1, 1),),
+    (),
+    (),
+    ((4, 0, 0, 1, 1), (4, 0, 0, 2, 1),),
+    ((4, 0, 1, 1, 0), (4, 0, 1, 2, 0),),
+    ((7, 1, 0, 1, 2, 1),),
+    (),
+    ((7, 1, 1, 0, 2, 0), (4, 0, 0, 3, 1),),
+    ((4, 0, 1, 1, 1),),
+    (),
+    ((7, 1, 1, 0, 3, 1), (7, 1, 0, 0, 1, 0), (4, 0, 1, 2, 1), (4, 0, 1, 3, 1),),
+    ((7, 1, 0, 0, 2, 1), (7, 1, 0, 1, 3, 1), (3, 0, 0, 3, 0), (7, 1, 0, 0, 3, 1), (7, 1, 0, 1, 2, 0), (7, 1, 1, 0, 3, 0), (3, 0, 1, 3, 0),),
+    ((4, 0, 1, 3, 0), (4, 0, 0, 3, 0),),
+    ((7, 1, 1, 1, 2, 1), (7, 1, 1, 1, 3, 1),),
+    (),
+    (),
+    ((7, 1, 0, 1, 3, 0), (7, 1, 0, 0, 2, 0),),
+    ((7, 1, 1, 1, 2, 0), (7, 1, 0, 0, 3, 0),),
+    (),
+    (),
+    (),
+    (),
+    (),
+    (),
+    ((13, 1, 3), (7, 1, 1, 1, 3, 0),),
+    (),
+    (),
+    (),
+    (),
+    (),
+    ((13, 1, 2),),
+    ((14, 1, 3, 0), (13, 1, 1),),
+    (),
+    ((13, 1, 0),),
+    (),
+    (),
+    ((13, 0, 3), (14, 1, 3, 1),),
+    ((13, 0, 2),),
     ((14, 1, 2, 0),),
-    (),
-    (),
-    ((13, 0, 3),),
-    ((14, 1, 3, 1),),
-    ((13, 0, 2), (13, 0, 1),),
-    (),
-    (),
-    (),
-    (),
-    (),
-    (),
-    (),
-    (),
-    (),
-    (),
-    (),
-    ((14, 0, 3, 0),),
+    ((13, 0, 1),),
+    (),
+    (),
+    (),
+    (),
+    (),
+    (),
     (),
     (),
     ((10, 4, 3),),
-    ((14, 1, 1, 0), (10, 0, 3),),
-    (),
-    ((14, 1, 2, 1), (14, 1, 1, 1), (14, 0, 2, 0), (10, 4, 2),),
-    ((14, 0, 3, 1), (10, 4, 1), (10, 1, 3),),
-    ((10, 4, 0),),
-    ((11, 4, 3),),
-    ((10, 2, 3), (10, 2, 2), (11, 4, 2), (10, 1, 2), (10, 1, 1), (14, 0, 1, 0),),
-    ((10, 2, 1), (11, 1, 3), (12, 4, 3, 0), (10, 1, 0),),
-    ((14, 1, 0, 0), (10, 0, 2), (11, 4, 1),),
-    ((13, 0, 0), (11, 4, 0),),
-    (),
-    (),
-    ((10, 2, 0), (11, 2, 3), (14, 1, 0, 1),),
-    ((11, 0, 3),),
-    ((14, 0, 2, 1), (11, 1, 2), (11, 2, 2),),
-    ((10, 3, 3), (10, 3, 2), (10, 3, 1),),
-    (),
-    (),
-    ((11, 1, 1), (12, 1, 3, 0), (10, 0, 1), (12, 4, 3, 1), (14, 0, 1, 1), (12, 4, 2, 0), (11, 0, 2), (12, 1, 2, 0), (11, 3, 3),),
-    (),
-    ((11, 2, 1), (12, 1, 3, 1), (12, 2, 3, 0), (11, 3, 2), (12, 2, 2, 0), (11, 3, 1), (12, 0, 3, 0), (12, 4, 2, 1), (12, 4, 1, 1),),
-    (),
-    ((10, 3, 0), (12, 1, 2, 1), (12, 3, 3, 0), (12, 2, 3, 1), (11, 2, 0), (12, 1, 1, 1), (12, 0, 2, 0), (10, 0, 0), (11, 1, 0), (12, 3, 2, 0),),
-    (),
-    ((12, 0, 3, 1), (11, 0, 1), (12, 4, 1, 0), (12, 3, 3, 1), (14, 0, 0, 0), (14, 0, 0, 1), (12, 2, 2, 1), (12, 2, 1, 0), (12, 2, 1, 1),),
-    (),
-    ((12, 3, 1, 0), (12, 1, 1, 0), (12, 3, 2, 1), (12, 3, 1, 1), (11, 3, 0), (11, 0, 0), (12, 0, 1, 0), (12, 0, 2, 1), (12, 0, 1, 1), (12, 1, 0, 0),),
-    (),
-    ((12, 4, 0, 1), (12, 2, 0, 0), (15, 0), (15, 1), (12, 1, 0, 1), (12, 4, 0, 0), (12, 3, 0, 0), (12, 2, 0, 1), (12, 3, 0, 1), (12, 0, 0, 1), (12, 0, 0, 0),),
+    (),
+    (),
+    ((10, 4, 2),),
+    ((10, 4, 1),),
+    (),
+    ((14, 1, 2, 1),),
+    (),
+    ((14, 0, 3, 0), (10, 0, 3),),
+    (),
+    ((14, 1, 1, 1), (14, 0, 2, 0),),
+    (),
+    ((10, 1, 3), (10, 1, 2), (10, 2, 3), (10, 2, 2), (10, 0, 2), (10, 4, 0), (10, 0, 1),),
+    ((14, 1, 1, 0), (11, 4, 3),),
+    ((11, 2, 3), (11, 2, 2), (11, 0, 3), (11, 4, 2), (11, 4, 1), (10, 2, 1),),
+    (),
+    ((11, 1, 3),),
+    (),
+    ((10, 1, 1), (11, 4, 0), (12, 4, 3, 0), (12, 4, 2, 0), (11, 0, 2),),
+    ((10, 2, 0), (10, 3, 3), (10, 3, 2), (14, 0, 3, 1), (14, 1, 0, 0), (13, 0, 0), (14, 0, 2, 1), (14, 1, 0, 1), (14, 0, 1, 0), (10, 3, 1),),
+    ((11, 1, 2), (10, 1, 0),),
+    (),
+    (),
+    (),
+    ((14, 0, 1, 1), (11, 1, 1), (12, 0, 3, 0), (11, 3, 3), (12, 1, 3, 0), (11, 2, 1), (12, 4, 3, 1), (12, 2, 3, 0),),
+    (),
+    ((11, 0, 1), (12, 0, 2, 0), (11, 3, 2), (12, 2, 2, 0), (12, 4, 2, 1), (12, 0, 3, 1), (11, 3, 1), (12, 1, 2, 0), (12, 1, 3, 1), (10, 0, 0),),
+    (),
+    ((12, 3, 3, 0), (14, 0, 0, 1), (10, 3, 0), (11, 2, 0), (12, 4, 1, 1), (12, 2, 3, 1), (12, 4, 1, 0), (14, 0, 0, 0), (12, 0, 2, 1), (12, 0, 1, 1), (12, 3, 2, 0),),
+    (),
+    ((12, 1, 2, 1), (12, 2, 1, 0), (12, 0, 1, 0), (12, 1, 1, 0), (12, 1, 1, 1), (12, 3, 3, 1), (11, 1, 0), (12, 2, 2, 1), (12, 2, 1, 1), (12, 3, 1, 0), (11, 0, 0),),
+    (),
+    ((11, 3, 0), (12, 3, 2, 1), (12, 3, 1, 1), (12, 1, 0, 0), (12, 4, 0, 0), (15, 1), (12, 2, 0, 0), (12, 4, 0, 1), (15, 0), (12, 0, 0, 0), (12, 0, 0, 1), (12, 1, 0, 1),),
+    (),
+    ((12, 3, 0, 0), (12, 2, 0, 1), (12, 3, 0, 1),),
 )
 BF, F32 = jnp.bfloat16, jnp.float32
 SUMS = ("bq", "bv", "bout", "bdown", "g1", "s1", "g2", "s2", "x", "mid", "res", "branch", "feed")
@@ -657,7 +689,7 @@
         c.start()
     enter(at)
     g = Gather(at, W, shard, PIECES, ag_send, ag_recv)
-    pg = PairGather(at, W, shard, ((UP, 1024), (DOWN, 1024)), (wup, wdown), pg_send, pg_recv)
+    pg = PairGather(at, W, shard, OVER_FIRST, ((UP, 1024), (DOWN, 1024)), (wup, wdown), pg_send, pg_recv)
     pltpu.make_async_copy(W.at[here, :], W.at[here, :], sem_in.at[0]).wait()
 
     home = {0: (W, DOWN, DOWN + 384), 1: (W, DOWN + 384, DOWN + 768), 2: (G3, 512, 896), 3: (W, OUT, OUT + 384), 4: (G3, 0, 512)}
@@ -685,7 +717,7 @@
         shares.append(share(2, dfeed, spot(x, t), at.across_x()))
 
     actions = {
-        0: g.line, 1: g.plane, 2: lambda m: pg.x_copy(m).start(), 3: pg.line, 4: pg.cross, 5: share_feed,
+        0: g.line, 1: g.plane, 2: lambda m: pg.x_copy(m).start(), 3: pg.line, 4: pg.cross, 5: share_feed, 6: pg.over, 7: pg.column_line,
         10: sc.begin, 11: sc.plane, 12: lambda p, k, w: sc.line(p, k, w, write(p)),
         13: ps.begin, 14: lambda m, k, w: ps.line(m, k, w, write_pair(m)), 15: lambda m: ps.last(m, write_pair(m)),
         16: ps.line_first, 17: lambda m: ps.meet(m, write_pair(m)),
@@ -963,7 +995,7 @@
     run(44)
     two.near()
     g.drain()
-    pg.drain(dfeed)
+    pg.drain(W.at[:, 0:2048])
 
     def grad_up(c):
         def part(d):
@@ -1192,7 +1224,7 @@
             dma((2,)),
             dma((5, 13)),
             dma((2,)),
-            dma((2, 10)),
+            dma((2, 19)),
             dma((1,)),
             dma((5, 13)),
             dma((1,)),

time: 180 us -> 180 us (level)
  no operation moved by 1% of the time
where the time goes in v1:
time: 180 us; the launch traced here: 179 us
  Pallas kernels  178 us (99%)
    pallas_call x1, Pallas kernels, block(): pl.pallas_call(block_kernel, out_shape=(jax.ShapeDtypeStruct((own, width)...  174 us
    pallas_call x1, Pallas kernels, close(): pl.pallas_call(close_kernel, out_shape=tuple((jax.ShapeDtypeStruct(a.shap...  4.64 us

profile of v1, /device:TPU:0, one launch (start us, length us, event | category | flops | bytes accessed | tf_op | source)
XLA Modules:
  0.0 179.3 jit_solution(44318454943984362)
XLA Ops:
  0.7 173.8 %shard_map.262 = (bf16[320,1024]{1,0:T(8,128)(2,1)}, f32[320,1024]{1,0:T(8,128)}, f32[3,64,512]{2,1,0:T(8,128)}, f32[64,512]{1,0:T(8,128)}, f32[64,2048]{1,0:T(8...) custom-call(s32[2]{0:T(128)} %counts.1, bf16[320,1024]{1,0:T(8,128)(2,1)} %x_hbm.1, bf16[320,1024]{1,0:T(8,128)(2,1)} %cot_hbm.1, ...), custom_call_target="tpu_custom_call" | custom-call | tf_op jit(solution)/shard_map/pallas_call | solution.py:1170
  174.5 4.6 %shard_map.263 = (bf16[320,1024]{1,0:T(8,128)(2,1)}, f32[320,1024]{1,0:T(8,128)}, f32[3,64,512]{2,1,0:T(8,128)}, f32[64,512]{1,0:T(8,128)}, f32[64,2048]{1,0:T(8...) custom-call(bf16[320,1024]{1,0:T(8,128)(2,1)} %get-tuple-element.37., ...), custom_call_target="tpu_custom_call" | custom-call | tf_op jit(solution)/shard_map/pallas_call | solution.py:1274

commit v2 on v1

--- a/solution.py
+++ b/solution.py
@@ -844,17 +844,13 @@
     run(18)
 
     def others(i, src, cols, k):
-        def body(c):
-            send_t[0, :, pl.ds(c, 512)] = nt(src[theirs, :], W[pl.ds(c, 512), cols]).astype(BF)
-        tiles(0, width, body, 512)
+        send_t[0] = nt(src[theirs, :], W[:, cols]).astype(BF)
         copy = send(i, send_t.at[0], got.at[k], at.twin())
         copy.start()
         return copy
 
     def owns(src, cols, keep):
-        def body(c):
-            keep[:, pl.ds(c, 512)] = nt(src[mine, :], W[pl.ds(c, 512), cols])
-        tiles(0, width, body, 512)
+        keep[...] = nt(src[mine, :], W[:, cols])
 
     branch_copy = others(3, heads, pl.ds(OUT, 512), 0)
     run(19)
@@ -1049,9 +1045,7 @@
     def grad_heads(p):
         ref, c0, c1 = home[p]
 
-        def body(c):
-            ref[pl.ds(c, 512), c0:c1] = tn(rows1[:, pl.ds(c, 512)], dproj[:, 384 * p : 384 * (p + 1)]).astype(BF)
-        tiles(0, width, body, 512)
+        ref[:, c0:c1] = tn(rows1[...], dproj[:, 384 * p : 384 * (p + 1)]).astype(BF)
 
     def attend_back(image, j):
         r = pl.ds(pl.multiple_of(image * own, own), own)

time: 180 us -> 179 us (level)
  no operation moved by 1% of the time
where the time goes in v2:
time: 179 us
  Pallas kernels  178 us (99%)
    pallas_call x1, Pallas kernels, block(): pl.pallas_call(block_kernel, out_shape=(jax.ShapeDtypeStruct((own, width)...  174 us
    pallas_call x1, Pallas kernels, close(): pl.pallas_call(close_kernel, out_shape=tuple((jax.ShapeDtypeStruct(a.shap...  4.64 us

profile of v2, /device:TPU:0, one launch (start us, length us, event | category | flops | bytes accessed | tf_op | source)
XLA Modules:
  0.0 179.2 jit_solution(821739532667548969)
XLA Ops:
  0.7 173.7 %shard_map.262 = (bf16[320,1024]{1,0:T(8,128)(2,1)}, f32[320,1024]{1,0:T(8,128)}, f32[3,64,512]{2,1,0:T(8,128)}, f32[64,512]{1,0:T(8,128)}, f32[64,2048]{1,0:T(8...) custom-call(s32[2]{0:T(128)} %counts.1, bf16[320,1024]{1,0:T(8,128)(2,1)} %x_hbm.1, bf16[320,1024]{1,0:T(8,128)(2,1)} %cot_hbm.1, ...), custom_call_target="tpu_custom_call" | custom-call | tf_op jit(solution)/shard_map/pallas_call | solution.py:1164
  174.3 4.6 %shard_map.263 = (bf16[320,1024]{1,0:T(8,128)(2,1)}, f32[320,1024]{1,0:T(8,128)}, f32[3,64,512]{2,1,0:T(8,128)}, f32[64,512]{1,0:T(8,128)}, f32[64,2048]{1,0:T(8...) custom-call(bf16[320,1024]{1,0:T(8,128)(2,1)} %get-tuple-element.37., ...), custom_call_target="tpu_custom_call" | custom-call | tf_op jit(solution)/shard_map/pallas_call | solution.py:1268
